TPU v7x, 32 devices: a whole 2x2x4 slice. The times are simulated.
32 devices in a mesh: gx: 2 (over x), gy: 4 (over y, core), gz: 4 (over z).
Axes of the slice: x: 2, y: 2, z: 4, core: 2. Of those that a mesh axis runs over, the one named last changes fastest.
Arguments:
- source: float32 [32, 128, 512], P('gx', 'gz', 'gy'), may hold values from -24 to 24
- conductance: float32 [32, 128, 512], P('gx', 'gz', 'gy'), may hold values from 0.5 to 4
- field_start: float32 [32, 128, 512], P('gx', 'gz', 'gy'), may hold values from -4 to 4
- panel_cell: int32 [3, 1024], P(None, ('gx', 'gy', 'gz')), may hold values from 0 to 511, as said below
- panel_area: float32 [1024], P(('gx', 'gy', 'gz')), may hold values from 0.5 to 2
Outputs:
- field: float32 [32, 128, 512], P('gx', 'gz', 'gy')
- potential: float32 [1024], P(('gx', 'gy', 'gz'))
Inputs may be any that keep to these rules, and one draw needn't show every extreme that they name: `panel_cell`: every column names a cell on the outer surface of the grid of 32 x 128 x 512 cells; several panels may share a cell; the panels are in no order of place.
All inputs are finite; a program needn't handle non-finite values.
Results may differ from a plain program's by a relative error of at most 0.0003.
Values sent between devices are 32-bit elements; how exact they have to be, the bound alone decides.
A program may use at most 64 MiB of HBM per device.

v0:
```python
import jax
import jax.numpy as jnp
from jax import lax
from jax.sharding import PartitionSpec as P

ROUNDS = 2
SWEEPS = 4


relax = 0.8


def extended(shard, sides, width):
    for axis, dim in sides:
        devices, length = (lax.axis_size(axis), shard.shape[dim])
        up = [(i, (i + 1) % devices) for i in range(devices - 1)]
        down = [(j, i) for i, j in up]
        last = lax.slice_in_dim(shard, length - width, length, axis=dim)
        initial = lax.slice_in_dim(shard, 0, width, axis=dim)
        before = lax.ppermute(last, axis, up)
        after = lax.ppermute(initial, axis, down)
        shard = jnp.concatenate([before, shard, after], axis=dim)
    return shard


def neighbours(array):
    return [
        array[2:, 1:-1, 1:-1],
        array[:-2, 1:-1, 1:-1],
        array[1:-1, 2:, 1:-1],
        array[1:-1, :-2, 1:-1],
        array[1:-1, 1:-1, 2:],
        array[1:-1, 1:-1, :-2],
    ]


def sweep(padded, coeff, load):
    center = padded[1:-1, 1:-1, 1:-1]
    middle = coeff[1:-1, 1:-1, 1:-1]
    diagonal = jnp.zeros_like(center)
    coupled = jnp.zeros_like(center)
    for value, other in zip(neighbours(padded), neighbours(coeff)):
        face_coeff = 0.5 * (middle + other)
        diagonal = diagonal + face_coeff
        coupled = coupled + face_coeff * value
    inside = middle > 0.0
    safe = jnp.where(inside, diagonal, 1.0)
    update = center + relax * (load - (diagonal * center - coupled)) / safe
    return jnp.where(inside, update, 0.0)


def block_kernel(targets, columns, weights):
    squared = jnp.zeros((targets.shape[1], columns.shape[1]), jnp.float32)
    for component in range(3):
        offset = targets[component][:, None] - columns[component][None, :]
        squared = squared + offset * offset
    kernel = lax.rsqrt(squared + 1.0)
    return jnp.dot(kernel, weights, precision=lax.Precision.HIGHEST)


def apply_kernel(targets, columns, weights):
    width = columns.shape[1]
    if width > 4096 and width % 4096 == 0:
        blocks = width // 4096
        column_blocks = columns.reshape(3, blocks, 4096).transpose(1, 0, 2)
        weight_blocks = weights.reshape(blocks, 4096)

        def advance(running, blocked):
            return (running + block_kernel(targets, blocked[0], blocked[1]), None)

        running, unused = lax.scan(
            advance, jnp.zeros((targets.shape[1],), jnp.float32), (column_blocks, weight_blocks)
        )
        return running
    return block_kernel(targets, columns, weights)


def shards(source, conductance, field_start, panel_cell, panel_area):
    size_x, size_y, size_z = field_start.shape
    own_xyz = panel_cell.astype(jnp.float32)
    own_rows = own_xyz.shape[1]
    listed = lax.all_gather(
        jnp.concatenate([own_xyz, panel_area[None, :]], 0), ("gx", "gy", "gz"), axis=1, tiled=True
    )
    all_xyz = listed[:3]
    all_area = listed[3]
    cells = all_xyz.astype(jnp.int32)
    local_x = cells[0] - lax.axis_index("gx") * size_x
    local_y = cells[1] - lax.axis_index("gz") * size_y
    local_z = cells[2] - lax.axis_index("gy") * size_z
    mine = (
        (local_x >= 0)
        & (local_x < size_x)
        & (local_y >= 0)
        & (local_y < size_y)
        & (local_z >= 0)
        & (local_z < size_z)
    )
    flat_index = jnp.where(mine, (local_x * size_y + local_y) * size_z + local_z, 0)
    coeff_one = extended(conductance, (("gx", 0), ("gy", 2), ("gz", 1)), 1)
    field = field_start
    potential = jnp.zeros((own_rows,), jnp.float32)
    for repeat in range(ROUNDS):
        picked = field.reshape(-1)[flat_index]
        weighted = jnp.where(mine, picked, 0.0) * all_area
        weights = lax.psum(weighted, ("gx", "gy", "gz"))
        potential = apply_kernel(own_xyz, all_xyz, weights)
        everywhere = lax.all_gather(potential, ("gx", "gy", "gz"), axis=0, tiled=True)
        added = jnp.where(mine, everywhere, 0.0)
        load = source.reshape(-1).at[flat_index].add(added).reshape(source.shape)
        for sweep_index in range(SWEEPS):
            padded = extended(field, (("gx", 0), ("gy", 2), ("gz", 1)), 1)
            field = sweep(padded, coeff_one, load)
    return (field, potential)


def solution(mesh):
    in_specs = (
        P("gx", "gz", "gy"),
        P("gx", "gz", "gy"),
        P("gx", "gz", "gy"),
        P(None, ("gx", "gy", "gz")),
        P(("gx", "gy", "gz")),
    )
    out_specs = (P("gx", "gz", "gy"), P(("gx", "gy", "gz")))
    return jax.shard_map(shards, mesh=mesh, in_specs=in_specs, out_specs=out_specs, check_vma=False)
```

profile of v0, /device:TPU:0, one launch (start us, length us, event | category | flops | bytes accessed | tf_op | source)
XLA Modules:
  0.0 469.8 jit_solution(7233386941538534285)
XLA Ops:
  1.7 4.8 %collective-permute-start.1 = (f32[1,32,128]{2,1,0:T(8,128)S(1)}, f32[1,32,128]{2,1,0:T(8,128)S(1)}, u32[]{:S(2)}, u32[]{:S(2)}) collective-permute-start(f32[1,32,128]{2,1,0:T(8,128)S(1)} %get-tuple-element.60), channel_id=1, source_target_pairs={{0,16},{1,17},{2,18},{3,19},{4,20},{5,21},{6,22},{7,23},{8,24},{9,... | collective-permute-start | bytes 49160 | tf_op jit(solution)/shard_map/ppermute | solution.py:20
  14.4 68.7 %all-gather = f32[32,32,4]{1,2,0:T(4,128)S(1)} all-gather(f32[1,32,4]{1,2,0:T(4,128)S(1)} %maximum_bitcast_fusion), channel_id=1, replica_groups=mesh['gx'=2,'gy'=4,'gz'=4] {'gx','gy','gz'}, dimensions={0}, use_global_device_ids=true | all-gather | bytes 16896 | tf_op jit(solution)/shard_map/all_gather | solution.py:82
  83.4 6.2 %gather_fusion = f32[1024]{0:T(1024)S(1)} fusion(f32[65536]{0:T(1024)S(1)} %bitcast.45, s32[1024]{0:T(1024)S(1)} %broadcast_clamp_fusion), kind=kCustom, calls=%fused_computation | custom fusion | bytes 12288 | tf_op jit(solution)/shard_map/gather | solution.py:104
  89.5 36.9 %psum.14 = f32[1024]{0:T(1024)S(1)} all-reduce(f32[1024]{0:T(1024)S(1)} %select_multiply_fusion.1), channel_id=1, replica_groups=mesh['gx'=2,'gy'=4,'gz'=4] {'gx','gy','gz'}, use_global_device_ids=true, to_apply=%region_0.1 | all-reduce | flops 1024 | bytes 8192 | tf_op jit(solution)/shard_map/psum | solution.py:106
  126.9 40.9 %all-reduce = f32[1024]{0:T(1024)S(1)} all-reduce(f32[1024]{0:T(1024)S(1)} %dynamic-update-slice), channel_id=1, replica_groups=mesh['gx'=2,'gy'=4,'gz'=4] {'gx','gy','gz'}, use_global_device_ids=true, to_apply=%add | all-reduce | flops 1024 | bytes 8192
  170.9 5.5 %collective-permute-start.8 = (f32[18,32,1]{2,1,0:T(8,128)S(1)}, f32[18,32,1]{2,1,0:T(8,128)S(1)}, u32[]{:S(2)}, u32[]{:S(2)}) collective-permute-start(f32[18,32,1]{2,1,0:T(8,128)S(1)} %get-tuple-element.45), channel_id=1, source_target_pairs={{0,4},{4,8},{8,12},{1,5},{5,9},{9,13},{2,6},{6,10},{10,14},{3,7},{... | collective-permute-start | bytes 6920 | tf_op jit(solution)/shard_map/ppermute | solution.py:20
  186.0 4.5 collective-permute-start.11
  190.6 7.4 %scatter_fusion = f32[65536]{0:T(1024)S(1)} fusion(f32[65536]{0:T(1024)S(1)} %bitcast.35, s32[1024]{0:T(1024)S(1)} %bitcast.49, f32[1024]{0:T(1024)S(1)} %broadcast_select_fusion.1), kind=kCustom, calls=%fused_computation.2 | custom fusion | flops 1024 | bytes 16384 | tf_op jit(solution)/shard_map/scatter-add | solution.py:110
  211.7 5.2 %collective-permute-done.15 = f32[18,32,1]{2,1,0:T(8,128)S(1)} collective-permute-done((f32[18,32,1]{2,1,0:T(8,128)S(1)}, f32[18,32,1]{2,1,0:T(8,128)S(1)}, u32[]{:S(2)}, u32[]{:S(2)}) %collective-permute-start.15) | collective-permute-done | bytes 2336 | tf_op jit(solution)/shard_map/ppermute | solution.py:21
  232.4 4.7 %collective-permute-start.20 = (f32[18,32,1]{2,1,0:T(8,128)S(1)}, f32[18,32,1]{2,1,0:T(8,128)S(1)}, u32[]{:S(2)}, u32[]{:S(2)}) collective-permute-start(f32[18,32,1]{2,1,0:T(8,128)S(1)} %get-tuple-element.39), channel_id=1, source_target_pairs={{0,4},{4,8},{8,12},{1,5},{5,9},{9,13},{2,6},{6,10},{10,14},{3,7},{... | collective-permute-start | bytes 6920 | tf_op jit(solution)/shard_map/ppermute | solution.py:20
  243.7 4.8 %collective-permute-start.23 = (f32[18,1,130]{2,1,0:T(1,128)S(1)}, f32[18,1,130]{2,1,0:T(1,128)S(1)}, u32[]{:S(2)}, u32[]{:S(2)}) collective-permute-start(f32[18,1,130]{2,1,0:T(1,128)S(1)} %get-tuple-element.21), channel_id=1, source_target_pairs={{0,1},{1,2},{2,3},{4,5},{5,6},{6,7},{8,9},{9,10},{10,11},{12,13},{... | collective-permute-start | bytes 28088 | tf_op jit(solution)/shard_map/ppermute | solution.py:20
  258.1 5.0 %collective-permute-start.26 = (f32[18,32,1]{2,1,0:T(8,128)S(1)}, f32[18,32,1]{2,1,0:T(8,128)S(1)}, u32[]{:S(2)}, u32[]{:S(2)}) collective-permute-start(f32[18,32,1]{2,1,0:T(8,128)S(1)} %get-tuple-element.37), channel_id=1, source_target_pairs={{0,4},{4,8},{8,12},{1,5},{5,9},{9,13},{2,6},{6,10},{10,14},{3,7},{... | collective-permute-start | bytes 6920 | tf_op jit(solution)/shard_map/ppermute | solution.py:20
  269.3 4.8 %collective-permute-start.29 = (f32[18,1,130]{2,1,0:T(1,128)S(1)}, f32[18,1,130]{2,1,0:T(1,128)S(1)}, u32[]{:S(2)}, u32[]{:S(2)}) collective-permute-start(f32[18,1,130]{2,1,0:T(1,128)S(1)} %get-tuple-element.19), channel_id=1, source_target_pairs={{0,1},{1,2},{2,3},{4,5},{5,6},{6,7},{8,9},{9,10},{10,11},{12,13},{... | collective-permute-start | bytes 28088 | tf_op jit(solution)/shard_map/ppermute | solution.py:20
  282.1 6.2 %gather_fusion.1 = f32[1024]{0:T(1024)S(1)} fusion(f32[65536]{0:T(1024)S(1)} %bitcast.44, s32[1024]{0:T(1024)S(1)} %broadcast_clamp_fusion), kind=kCustom, calls=%fused_computation.1 | custom fusion | bytes 12288 | tf_op jit(solution)/shard_map/gather | solution.py:104
  288.3 43.7 %psum.15 = f32[1024]{0:T(1024)S(1)} all-reduce(f32[1024]{0:T(1024)S(1)} %select_multiply_fusion), channel_id=1, replica_groups=mesh['gx'=2,'gy'=4,'gz'=4] {'gx','gy','gz'}, use_global_device_ids=true, to_apply=%region_2.3 | all-reduce | flops 1024 | bytes 8192 | tf_op jit(solution)/shard_map/psum | solution.py:106
  335.8 44.9 %all-reduce.1 = f32[1024]{0:T(1024)S(1)} all-reduce(f32[1024]{0:T(1024)S(1)} %dynamic-update-slice.1), channel_id=1, replica_groups=mesh['gx'=2,'gy'=4,'gz'=4] {'gx','gy','gz'}, use_global_device_ids=true, to_apply=%add.1 | all-reduce | flops 1024 | bytes 8192
  382.2 4.5 collective-permute-start.35
  386.7 7.4 %scatter_fusion.1 = f32[65536]{0:T(1024)S(1)} fusion(f32[65536]{0:T(1024)S(1)} %copy.16, s32[1024]{0:T(1024)S(1)} %bitcast.50, f32[1024]{0:T(1024)S(1)} %broadcast_select_fusion), kind=kCustom, calls=%fused_computation.3 | custom fusion | flops 1024 | bytes 16384 | tf_op jit(solution)/shard_map/scatter-add | solution.py:110
  404.9 4.8 %collective-permute-done.39 = f32[18,32,1]{2,1,0:T(8,128)S(1)} collective-permute-done((f32[18,32,1]{2,1,0:T(8,128)S(1)}, f32[18,32,1]{2,1,0:T(8,128)S(1)}, u32[]{:S(2)}, u32[]{:S(2)}) %collective-permute-start.39) | collective-permute-done | bytes 2336 | tf_op jit(solution)/shard_map/ppermute | solution.py:21
  411.2 4.5 collective-permute-start.41
  425.2 4.7 %collective-permute-start.44 = (f32[18,32,1]{2,1,0:T(8,128)S(1)}, f32[18,32,1]{2,1,0:T(8,128)S(1)}, u32[]{:S(2)}, u32[]{:S(2)}) collective-permute-start(f32[18,32,1]{2,1,0:T(8,128)S(1)} %get-tuple-element.31), channel_id=1, source_target_pairs={{0,4},{4,8},{8,12},{1,5},{5,9},{9,13},{2,6},{6,10},{10,14},{3,7},{... | collective-permute-start | bytes 6920 | tf_op jit(solution)/shard_map/ppermute | solution.py:20
  436.5 4.8 %collective-permute-start.47 = (f32[18,1,130]{2,1,0:T(1,128)S(1)}, f32[18,1,130]{2,1,0:T(1,128)S(1)}, u32[]{:S(2)}, u32[]{:S(2)}) collective-permute-start(f32[18,1,130]{2,1,0:T(1,128)S(1)} %get-tuple-element.13), channel_id=1, source_target_pairs={{0,1},{1,2},{2,3},{4,5},{5,6},{6,7},{8,9},{9,10},{10,11},{12,13},{... | collective-permute-start | bytes 28088 | tf_op jit(solution)/shard_map/ppermute | solution.py:20
  450.9 5.0 %collective-permute-start.50 = (f32[18,32,1]{2,1,0:T(8,128)S(1)}, f32[18,32,1]{2,1,0:T(8,128)S(1)}, u32[]{:S(2)}, u32[]{:S(2)}) collective-permute-start(f32[18,32,1]{2,1,0:T(8,128)S(1)} %get-tuple-element.29), channel_id=1, source_target_pairs={{0,4},{4,8},{8,12},{1,5},{5,9},{9,13},{2,6},{6,10},{10,14},{3,7},{... | collective-permute-start | bytes 6920 | tf_op jit(solution)/shard_map/ppermute | solution.py:20
  462.2 4.8 %collective-permute-start.53 = (f32[18,1,130]{2,1,0:T(1,128)S(1)}, f32[18,1,130]{2,1,0:T(1,128)S(1)}, u32[]{:S(2)}, u32[]{:S(2)}) collective-permute-start(f32[18,1,130]{2,1,0:T(1,128)S(1)} %get-tuple-element.11), channel_id=1, source_target_pairs={{0,1},{1,2},{2,3},{4,5},{5,6},{6,7},{8,9},{9,10},{10,11},{12,13},{... | collective-permute-start | bytes 28088 | tf_op jit(solution)/shard_map/ppermute | solution.py:20
  (177 shorter events, 133.0 us)
Async XLA Ops:
  1.7 166.2 %collective-permute-start.1 = (f32[1,32,128]{2,1,0:T(8,128)S(1)}, f32[1,32,128]{2,1,0:T(8,128)S(1)}, u32[]{:S(2)}, u32[]{:S(2)}) collective-permute-start(f32[1,32,128]{2,1,0:T(8,128)S(1)} %get-tuple-element.60), channel_id=1, source_target_pairs={{0,16},{1,17},{2,18},{3,19},{4,20},{5,21},{6,22},{7,23},{8,24},{9,... | collective-permute-start | bytes 49160 | tf_op jit(solution)/shard_map/ppermute | solution.py:20
  6.5 161.4 %collective-permute-start = (f32[1,32,128]{2,1,0:T(8,128)S(1)}, f32[1,32,128]{2,1,0:T(8,128)S(1)}, u32[]{:S(2)}, u32[]{:S(2)}) collective-permute-start(f32[1,32,128]{2,1,0:T(8,128)S(1)} %get-tuple-element.61), channel_id=1, source_target_pairs={{16,0},{17,1},{18,2},{19,3},{20,4},{21,5},{22,6},{23,7},{24,8},{25... | collective-permute-start | bytes 49160 | tf_op jit(solution)/shard_map/ppermute | solution.py:21
  7.8 162.9 %collective-permute-start.7 = (f32[1,32,128]{2,1,0:T(8,128)S(1)}, f32[1,32,128]{2,1,0:T(8,128)S(1)}, u32[]{:S(2)}, u32[]{:S(2)}) collective-permute-start(f32[1,32,128]{2,1,0:T(8,128)S(1)} %get-tuple-element.63), channel_id=1, source_target_pairs={{0,16},{1,17},{2,18},{3,19},{4,20},{5,21},{6,22},{7,23},{8,24},{9,... | collective-permute-start | bytes 49160 | tf_op jit(solution)/shard_map/ppermute | solution.py:20
  12.4 158.4 %collective-permute-start.6 = (f32[1,32,128]{2,1,0:T(8,128)S(1)}, f32[1,32,128]{2,1,0:T(8,128)S(1)}, u32[]{:S(2)}, u32[]{:S(2)}) collective-permute-start(f32[1,32,128]{2,1,0:T(8,128)S(1)} %get-tuple-element.62), channel_id=1, source_target_pairs={{16,0},{17,1},{18,2},{19,3},{20,4},{21,5},{22,6},{23,7},{24,8},{25... | collective-permute-start | bytes 49160 | tf_op jit(solution)/shard_map/ppermute | solution.py:21
  168.1 9.7 %collective-permute-start.2 = (f32[18,32,1]{2,1,0:T(8,128)S(1)}, f32[18,32,1]{2,1,0:T(8,128)S(1)}, u32[]{:S(2)}, u32[]{:S(2)}) collective-permute-start(f32[18,32,1]{2,1,0:T(8,128)S(1)} %get-tuple-element.42), channel_id=1, source_target_pairs={{0,4},{4,8},{8,12},{1,5},{5,9},{9,13},{2,6},{6,10},{10,14},{3,7},{... | collective-permute-start | bytes 6920 | tf_op jit(solution)/shard_map/ppermute | solution.py:20
  169.4 8.4 %collective-permute-start.3 = (f32[18,32,1]{2,1,0:T(8,128)S(1)}, f32[18,32,1]{2,1,0:T(8,128)S(1)}, u32[]{:S(2)}, u32[]{:S(2)}) collective-permute-start(f32[18,32,1]{2,1,0:T(8,128)S(1)} %get-tuple-element.43), channel_id=1, source_target_pairs={{4,0},{8,4},{12,8},{5,1},{9,5},{13,9},{6,2},{10,6},{14,10},{7,3},{... | collective-permute-start | bytes 6920 | tf_op jit(solution)/shard_map/ppermute | solution.py:21
  170.9 12.9 %collective-permute-start.8 = (f32[18,32,1]{2,1,0:T(8,128)S(1)}, f32[18,32,1]{2,1,0:T(8,128)S(1)}, u32[]{:S(2)}, u32[]{:S(2)}) collective-permute-start(f32[18,32,1]{2,1,0:T(8,128)S(1)} %get-tuple-element.45), channel_id=1, source_target_pairs={{0,4},{4,8},{8,12},{1,5},{5,9},{9,13},{2,6},{6,10},{10,14},{3,7},{... | collective-permute-start | bytes 6920 | tf_op jit(solution)/shard_map/ppermute | solution.py:20
  176.5 7.4 %collective-permute-start.9 = (f32[18,32,1]{2,1,0:T(8,128)S(1)}, f32[18,32,1]{2,1,0:T(8,128)S(1)}, u32[]{:S(2)}, u32[]{:S(2)}) collective-permute-start(f32[18,32,1]{2,1,0:T(8,128)S(1)} %get-tuple-element.44), channel_id=1, source_target_pairs={{4,0},{8,4},{12,8},{5,1},{9,5},{13,9},{6,2},{10,6},{14,10},{7,3},{... | collective-permute-start | bytes 6920 | tf_op jit(solution)/shard_map/ppermute | solution.py:21
  178.0 20.0 %collective-permute-start.4 = (f32[18,1,130]{2,1,0:T(1,128)S(1)}, f32[18,1,130]{2,1,0:T(1,128)S(1)}, u32[]{:S(2)}, u32[]{:S(2)}) collective-permute-start(f32[18,1,130]{2,1,0:T(1,128)S(1)} %get-tuple-element.25), channel_id=1, source_target_pairs={{1,0},{2,1},{3,2},{5,4},{6,5},{7,6},{9,8},{10,9},{11,10},{13,12},{... | collective-permute-start | bytes 28088 | tf_op jit(solution)/shard_map/ppermute | solution.py:21
  179.3 18.8 %collective-permute-start.5 = (f32[18,1,130]{2,1,0:T(1,128)S(1)}, f32[18,1,130]{2,1,0:T(1,128)S(1)}, u32[]{:S(2)}, u32[]{:S(2)}) collective-permute-start(f32[18,1,130]{2,1,0:T(1,128)S(1)} %get-tuple-element.24), channel_id=1, source_target_pairs={{0,1},{1,2},{2,3},{4,5},{5,6},{6,7},{8,9},{9,10},{10,11},{12,13},{... | collective-permute-start | bytes 28088 | tf_op jit(solution)/shard_map/ppermute | solution.py:20
  184.7 13.3 %collective-permute-start.10 = (f32[18,1,130]{2,1,0:T(1,128)S(1)}, f32[18,1,130]{2,1,0:T(1,128)S(1)}, u32[]{:S(2)}, u32[]{:S(2)}) collective-permute-start(f32[18,1,130]{2,1,0:T(1,128)S(1)} %get-tuple-element.26), channel_id=1, source_target_pairs={{1,0},{2,1},{3,2},{5,4},{6,5},{7,6},{9,8},{10,9},{11,10},{13,12},{... | collective-permute-start | bytes 28088 | tf_op jit(solution)/shard_map/ppermute | solution.py:21
  186.0 12.1 %collective-permute-start.11 = (f32[18,1,130]{2,1,0:T(1,128)S(1)}, f32[18,1,130]{2,1,0:T(1,128)S(1)}, u32[]{:S(2)}, u32[]{:S(2)}) collective-permute-start(f32[18,1,130]{2,1,0:T(1,128)S(1)} %get-tuple-element.27), channel_id=1, source_target_pairs={{0,1},{1,2},{2,3},{4,5},{5,6},{6,7},{8,9},{9,10},{10,11},{12,13},{... | collective-permute-start | bytes 28088 | tf_op jit(solution)/shard_map/ppermute | solution.py:20
  210.4 6.5 %collective-permute-start.15 = (f32[18,32,1]{2,1,0:T(8,128)S(1)}, f32[18,32,1]{2,1,0:T(8,128)S(1)}, u32[]{:S(2)}, u32[]{:S(2)}) collective-permute-start(f32[18,32,1]{2,1,0:T(8,128)S(1)} %get-tuple-element.40), channel_id=1, source_target_pairs={{4,0},{8,4},{12,8},{5,1},{9,5},{13,9},{6,2},{10,6},{14,10},{7,3},{... | collective-permute-start | bytes 6920 | tf_op jit(solution)/shard_map/ppermute | solution.py:21
  243.7 6.3 %collective-permute-start.23 = (f32[18,1,130]{2,1,0:T(1,128)S(1)}, f32[18,1,130]{2,1,0:T(1,128)S(1)}, u32[]{:S(2)}, u32[]{:S(2)}) collective-permute-start(f32[18,1,130]{2,1,0:T(1,128)S(1)} %get-tuple-element.21), channel_id=1, source_target_pairs={{0,1},{1,2},{2,3},{4,5},{5,6},{6,7},{8,9},{9,10},{10,11},{12,13},{... | collective-permute-start | bytes 28088 | tf_op jit(solution)/shard_map/ppermute | solution.py:20
  258.1 6.3 %collective-permute-start.26 = (f32[18,32,1]{2,1,0:T(8,128)S(1)}, f32[18,32,1]{2,1,0:T(8,128)S(1)}, u32[]{:S(2)}, u32[]{:S(2)}) collective-permute-start(f32[18,32,1]{2,1,0:T(8,128)S(1)} %get-tuple-element.37), channel_id=1, source_target_pairs={{0,4},{4,8},{8,12},{1,5},{5,9},{9,13},{2,6},{6,10},{10,14},{3,7},{... | collective-permute-start | bytes 6920 | tf_op jit(solution)/shard_map/ppermute | solution.py:20
  269.3 6.3 %collective-permute-start.29 = (f32[18,1,130]{2,1,0:T(1,128)S(1)}, f32[18,1,130]{2,1,0:T(1,128)S(1)}, u32[]{:S(2)}, u32[]{:S(2)}) collective-permute-start(f32[18,1,130]{2,1,0:T(1,128)S(1)} %get-tuple-element.19), channel_id=1, source_target_pairs={{0,1},{1,2},{2,3},{4,5},{5,6},{6,7},{8,9},{9,10},{10,11},{12,13},{... | collective-permute-start | bytes 28088 | tf_op jit(solution)/shard_map/ppermute | solution.py:20
  276.3 55.7 %collective-permute-start.30 = (f32[1,32,128]{2,1,0:T(8,128)S(1)}, f32[1,32,128]{2,1,0:T(8,128)S(1)}, u32[]{:S(2)}, u32[]{:S(2)}) collective-permute-start(f32[1,32,128]{2,1,0:T(8,128)S(1)} %get-tuple-element.53), channel_id=1, source_target_pairs={{16,0},{17,1},{18,2},{19,3},{20,4},{21,5},{22,6},{23,7},{24,8},{25... | collective-permute-start | bytes 49160 | tf_op jit(solution)/shard_map/ppermute | solution.py:21
  277.6 54.4 %collective-permute-start.31 = (f32[1,32,128]{2,1,0:T(8,128)S(1)}, f32[1,32,128]{2,1,0:T(8,128)S(1)}, u32[]{:S(2)}, u32[]{:S(2)}) collective-permute-start(f32[1,32,128]{2,1,0:T(8,128)S(1)} %get-tuple-element.52), channel_id=1, source_target_pairs={{0,16},{1,17},{2,18},{3,19},{4,20},{5,21},{6,22},{7,23},{8,24},{9,... | collective-permute-start | bytes 49160 | tf_op jit(solution)/shard_map/ppermute | solution.py:20
  332.2 48.5 %collective-permute-start.32 = (f32[18,32,1]{2,1,0:T(8,128)S(1)}, f32[18,32,1]{2,1,0:T(8,128)S(1)}, u32[]{:S(2)}, u32[]{:S(2)}) collective-permute-start(f32[18,32,1]{2,1,0:T(8,128)S(1)} %get-tuple-element.35), channel_id=1, source_target_pairs={{0,4},{4,8},{8,12},{1,5},{5,9},{9,13},{2,6},{6,10},{10,14},{3,7},{... | collective-permute-start | bytes 6920 | tf_op jit(solution)/shard_map/ppermute | solution.py:20
  333.5 47.2 %collective-permute-start.33 = (f32[18,32,1]{2,1,0:T(8,128)S(1)}, f32[18,32,1]{2,1,0:T(8,128)S(1)}, u32[]{:S(2)}, u32[]{:S(2)}) collective-permute-start(f32[18,32,1]{2,1,0:T(8,128)S(1)} %get-tuple-element.34), channel_id=1, source_target_pairs={{4,0},{8,4},{12,8},{5,1},{9,5},{13,9},{6,2},{10,6},{14,10},{7,3},{... | collective-permute-start | bytes 6920 | tf_op jit(solution)/shard_map/ppermute | solution.py:21
  380.9 13.3 %collective-permute-start.34 = (f32[18,1,130]{2,1,0:T(1,128)S(1)}, f32[18,1,130]{2,1,0:T(1,128)S(1)}, u32[]{:S(2)}, u32[]{:S(2)}) collective-permute-start(f32[18,1,130]{2,1,0:T(1,128)S(1)} %get-tuple-element.16), channel_id=1, source_target_pairs={{1,0},{2,1},{3,2},{5,4},{6,5},{7,6},{9,8},{10,9},{11,10},{13,12},{... | collective-permute-start | bytes 28088 | tf_op jit(solution)/shard_map/ppermute | solution.py:21
  382.2 12.0 %collective-permute-start.35 = (f32[18,1,130]{2,1,0:T(1,128)S(1)}, f32[18,1,130]{2,1,0:T(1,128)S(1)}, u32[]{:S(2)}, u32[]{:S(2)}) collective-permute-start(f32[18,1,130]{2,1,0:T(1,128)S(1)} %get-tuple-element.17), channel_id=1, source_target_pairs={{0,1},{1,2},{2,3},{4,5},{5,6},{6,7},{8,9},{9,10},{10,11},{12,13},{... | collective-permute-start | bytes 28088 | tf_op jit(solution)/shard_map/ppermute | solution.py:20
  436.5 6.3 %collective-permute-start.47 = (f32[18,1,130]{2,1,0:T(1,128)S(1)}, f32[18,1,130]{2,1,0:T(1,128)S(1)}, u32[]{:S(2)}, u32[]{:S(2)}) collective-permute-start(f32[18,1,130]{2,1,0:T(1,128)S(1)} %get-tuple-element.13), channel_id=1, source_target_pairs={{0,1},{1,2},{2,3},{4,5},{5,6},{6,7},{8,9},{9,10},{10,11},{12,13},{... | collective-permute-start | bytes 28088 | tf_op jit(solution)/shard_map/ppermute | solution.py:20
  450.9 6.3 %collective-permute-start.50 = (f32[18,32,1]{2,1,0:T(8,128)S(1)}, f32[18,32,1]{2,1,0:T(8,128)S(1)}, u32[]{:S(2)}, u32[]{:S(2)}) collective-permute-start(f32[18,32,1]{2,1,0:T(8,128)S(1)} %get-tuple-element.29), channel_id=1, source_target_pairs={{0,4},{4,8},{8,12},{1,5},{5,9},{9,13},{2,6},{6,10},{10,14},{3,7},{... | collective-permute-start | bytes 6920 | tf_op jit(solution)/shard_map/ppermute | solution.py:20
  (37 other events, 186.8 us)
where the time goes:
time: 477 us; the launch traced here: 470 us
  blocking collectives  235 us (49%)
  starting transfers between devices  150 us (31%)
  waiting for transfers between devices  41.6 us (9%)
  other arithmetic  24 us (5%)
  local copies, waits for them, and re-layouts  17.1 us (4%)
    ppermute x27, starting transfers between devices, extended(): before = lax.ppermute(last, axis, up)  115 us
    unnamed x2, blocking collectives  85.8 us
    psum x2, blocking collectives, shards(): weights = lax.psum(weighted, ('gx', 'gy', 'gz'))  80.6 us
    all_gather x1, blocking collectives, shards(): lax.all_gather(jnp.concatenate([own_xyz, panel_area[None, :]], 0), ('gx',...  68.7 us
    ppermute x27, starting transfers between devices, extended(): after = lax.ppermute(initial, axis, down)  34.9 us
    ppermute x27, waiting for transfers between devices, extended(): after = lax.ppermute(initial, axis, down)  24.5 us
    ppermute x27, waiting for transfers between devices, extended(): before = lax.ppermute(last, axis, up)  17.1 us
    scatter-add x2, other arithmetic, shards(): load = source.reshape(-1).at[flat_index].add(added).reshape(source.shape)  14.9 us
  transfers between devices with their start and end apart: 54, of which 18 were waited for; matrix products, arithmetic and copies ran while one was open for 6% of the time, Pallas kernels for 0%

commit v1 on v0

v1 whole, which is shorter than its diff:
```python
import functools

import jax
import jax.numpy as jnp
from jax import lax
from jax.experimental import pallas as pl
from jax.experimental.pallas import tpu as pltpu
from jax.sharding import PartitionSpec as P

ROUNDS = 2
SWEEPS = 4
W = SWEEPS
relax = 0.8
MESH = pl.DeviceIdType.MESH
F32 = jnp.float32
BF16 = jnp.bfloat16


def split2(value):
    high = value.astype(BF16)
    low = (value - high.astype(F32)).astype(BF16)
    return high, low


def split3(value):
    high = value.astype(BF16)
    rest = value - high.astype(F32)
    mid = rest.astype(BF16)
    low = (rest - mid.astype(F32)).astype(BF16)
    return high, mid, low


def kernel(
    cfg, panel_ref, field_ref, source_ref, cond_ref, out_ref, pot_ref,
    ext, ext2, ping, pong, coef, inv, load, yrecv, yrecv2, zsend, zsend2, zrecv, zrecv2,
    ag1_send, ag1, ag_own, cells, ws1_send, ws1, ws2_send, ws2, cols, onehot, onehot_ext, spread, kmat,
    local_sem, ag1_ss, ag1_rs, ag2_ss, ag2_rs, h1_ss, h1_rs, h2_ss, h2_rs, w1_ss, w1_rs, w2_ss, w2_rs,
):
    gxn, gyn, gzn, sx, sy, sz, own, count = cfg
    q_count = gxn * gyn
    width = own * gzn
    ex, ey, ez = sx + 2 * W, sy + 8, 2 * sz
    rows = ex * ey
    rows_pad = zsend.shape[-1]
    gx, gy, gz = lax.axis_index("gx"), lax.axis_index("gy"), lax.axis_index("gz")
    q = gx * gyn + gy

    locals_ = []
    for a, ref in enumerate((field_ref, source_ref, cond_ref)):
        copy = pltpu.make_async_copy(ref, ext.at[a, W : W + sx, 0:sy, 0:sz], local_sem.at[a])
        copy.start()
        locals_.append(copy)

    for a in range(3):
        ext[a, 0:W, :, 0:sz] = jnp.zeros((W, ey, sz), F32)
        ext[a, W + sx :, :, 0:sz] = jnp.zeros((W, ey, sz), F32)
    ext2[0, 0:W, :, 0:sz] = jnp.zeros((W, ey, sz), F32)
    ext2[0, W + sx :, :, 0:sz] = jnp.zeros((W, ey, sz), F32)
    yrecv[...] = jnp.zeros(yrecv.shape, F32)
    yrecv2[...] = jnp.zeros(yrecv2.shape, F32)
    zrecv[...] = jnp.zeros(zrecv.shape, F32)
    zrecv2[...] = jnp.zeros(zrecv2.shape, F32)

    def z_peer(offset):
        return (gx, gy, lax.rem(gz + offset, gzn))

    def q_peer(offset):
        other = lax.rem(q + offset, q_count)
        return (other // gyn, lax.rem(other, gyn), gz)

    def in_grid(dx, dy):
        ok = None
        for step, index, size in ((dx, gx, gxn), (dy, gz, gzn)):
            if step:
                test = index < size - 1 if step > 0 else index > 0
                ok = test if ok is None else jnp.logical_and(ok, test)
        return ok

    barrier = pltpu.get_barrier_semaphore()
    total = jnp.int32(gzn - 1 + q_count - 1)
    for offset in range(1, gzn):
        pl.semaphore_signal(barrier, inc=1, device_id=z_peer(offset), device_id_type=MESH)
    for offset in range(1, q_count):
        pl.semaphore_signal(barrier, inc=1, device_id=q_peer(offset), device_id_type=MESH)
    for dx in (-1, 1):
        for dy in (-1, 1):
            ok = in_grid(dx, dy)
            total = total + jnp.where(ok, 1, 0).astype(jnp.int32)

            @pl.when(ok)
            def _():
                pl.semaphore_signal(barrier, inc=1, device_id=(gx + dx, gy, gz + dy), device_id_type=MESH)

    lane_w = lax.broadcasted_iota(jnp.int32, (8, width), 1)
    mine_lanes = jnp.logical_and(lane_w >= gz * own, lane_w < (gz + 1) * own)
    own_tile = jnp.where(mine_lanes, panel_ref[...], 0.0)
    ag1_send[...] = own_tile
    pl.semaphore_wait(barrier, total)

    def exchange_z(src, dst, ss, rs):
        copies = []
        for offset in range(1, gzn):
            copy = pltpu.make_async_remote_copy(
                src_ref=src, dst_ref=dst.at[offset - 1], send_sem=ss.at[offset - 1], recv_sem=rs.at[offset - 1],
                device_id=z_peer(offset), device_id_type=MESH,
            )
            copy.start()
            copies.append(copy)
        return copies

    ag1_copies = exchange_z(ag1_send, ag1, ag1_ss, ag1_rs)
    for copy in locals_:
        copy.wait()

    directions = [(dx, dy) for dx in (-1, 0, 1) for dy in (-1, 0, 1) if dx or dy]

    def halo_copies(base, yr, ss, rs):
        made = []
        for n, (dx, dy) in enumerate(directions):
            xs = {-1: pl.ds(W, W), 0: pl.ds(W, sx), 1: pl.ds(sx, W)}[dx]
            ys = {-1: pl.ds(0, 8), 0: pl.ds(0, sy), 1: pl.ds(sy - 8, 8)}[dy]
            xd = {-1: pl.ds(W + sx, W), 0: pl.ds(W, sx), 1: pl.ds(0, W)}[dx]
            src = base.at[:, xs, ys, pl.ds(0, sz)]
            if dy == 0:
                dst = base.at[:, xd, pl.ds(0, sy), pl.ds(0, sz)]
            else:
                dst = yr.at[0 if dy < 0 else 1, :, xd]
            made.append(
                (
                    pltpu.make_async_remote_copy(
                        src_ref=src, dst_ref=dst, send_sem=ss.at[n], recv_sem=rs.at[n],
                        device_id=(gx + dx, gy, gz + dy), device_id_type=MESH,
                    ),
                    in_grid(dx, dy),
                    in_grid(-dx, -dy),
                )
            )
        return made

    def start_halo(made):
        for copy, to, _ in made:
            pl.when(to)(copy.start)

    def wait_halo(made):
        for copy, to, origin in made:
            pl.when(origin)(copy.wait_recv)
        for copy, to, origin in made:
            pl.when(to)(copy.wait_send)

    h1 = halo_copies(ext, yrecv, h1_ss.at[0], h1_rs.at[0])
    start_halo(h1)

    tile = own_tile
    for n, copy in enumerate(ag1_copies):
        copy.wait_recv()
        tile = tile + ag1[n]
    ag_own[...] = tile
    ag2_copies = []
    for offset in range(1, q_count):
        copy = pltpu.make_async_remote_copy(
            src_ref=ag_own, dst_ref=cells.at[q], send_sem=ag2_ss.at[offset - 1], recv_sem=ag2_rs.at[offset - 1],
            device_id=q_peer(offset), device_id_type=MESH,
        )
        copy.start()
        ag2_copies.append(copy)
    cells[q] = tile

    def brick_transposed(base):
        return base[0, W : W + sx, 0:sy, 0:sz].reshape(sx * sy, sz).T

    f_t = brick_transposed(ext)

    for copy in ag2_copies:
        copy.wait_recv()

    listed = jnp.concatenate([cells[n] for n in range(q_count)], axis=1)
    cell_x = listed[0:1].astype(jnp.int32) - gx * sx
    cell_y = listed[1:2].astype(jnp.int32) - gz * sy
    cell_z = listed[2:3].astype(jnp.int32) - gy * sz
    area = listed[3:4]
    inside = (cell_x >= 0) & (cell_x < sx) & (cell_y >= 0) & (cell_y < sy) & (cell_z >= 0) & (cell_z < sz)
    row_id = jnp.where(inside, cell_x * sy + cell_y, -1)
    near = (cell_x >= -W) & (cell_x < sx + W) & (cell_y >= -W) & (cell_y < sy + W) & (cell_z >= -W) & (cell_z < sz + W)
    row_ext = jnp.where(near, (cell_x + W) * ey + jnp.where(cell_y < 0, cell_y + ey, cell_y), -1)

    def fill_onehot(ref, ids, block):
        def body(i, _):
            start = pl.multiple_of(i * block, block)
            sub = lax.broadcasted_iota(jnp.int32, (block, count), 0) + start
            ref[pl.ds(start, block), :] = jnp.where(sub == ids, 1.0, 0.0).astype(BF16)
            return 0

        lax.fori_loop(0, ref.shape[0] // block, body, 0)

    fill_onehot(onehot, row_id, 32)

    block_j = 512

    def gather_weights(f_t, send):
        parts = jnp.concatenate(split3(f_t), axis=0)
        pieces = []
        for start in range(0, count, block_j):
            got = jnp.dot(parts, onehot[:, start : start + block_j], preferred_element_type=F32)
            value = got[0:sz] + got[sz : 2 * sz] + got[2 * sz :]
            sub = lax.broadcasted_iota(jnp.int32, (sz, block_j), 0)
            value = jnp.where(sub == cell_z[:, start : start + block_j], value, 0.0)
            pieces.append(jnp.sum(value, axis=0, keepdims=True) * area[:, start : start + block_j])
        row = jnp.concatenate(pieces, axis=1)
        for n in range(q_count):
            send[n : n + 1, :] = row[:, n * width : (n + 1) * width]

    def w_stage2(r, copies1):
        value = ws1_send[r]
        for n, copy in enumerate(copies1):
            copy.wait_recv()
            value = value + ws1[r, n]
        ws2_send[r] = value
        copies = []
        for offset in range(1, q_count):
            copy = pltpu.make_async_remote_copy(
                src_ref=ws2_send.at[r], dst_ref=ws2.at[r, offset - 1],
                send_sem=w2_ss.at[r, offset - 1], recv_sem=w2_rs.at[r, offset - 1],
                device_id=q_peer(offset), device_id_type=MESH,
            )
            copy.start()
            copies.append(copy)
        return copies

    def w_total(r, copies2):
        value = ws2_send[r]
        for n, copy in enumerate(copies2):
            copy.wait_recv()
            value = value + ws2[r, n]
        return jnp.concatenate([value[n : n + 1] for n in range(q_count)], axis=1)

    sub8 = lax.broadcasted_iota(jnp.int32, (8, sz), 0)

    def fill_y(base, yr, arrays):
        for a in range(arrays):
            base[a, :, sy:, 0:sz] = jnp.where(sub8[None] < W, yr[0, a], yr[1, a])

    def z_copies(base, zs, zr, arrays, ss, rs):
        for a in range(arrays):
            flat = base[a, :, :, 0:sz].reshape(rows, sz)
            if rows_pad > rows:
                flat = jnp.concatenate([flat, jnp.zeros((rows_pad - rows, sz), F32)], axis=0)
            turned = flat.T
            zs[0, a] = turned[0:8]
            zs[1, a] = turned[sz - 8 :]
        made = []
        for n, step in enumerate((-1, 1)):
            to = gy > 0 if step < 0 else gy < gyn - 1
            origin = gy < gyn - 1 if step < 0 else gy > 0
            copy = pltpu.make_async_remote_copy(
                src_ref=zs.at[n], dst_ref=zr.at[n], send_sem=ss.at[n], recv_sem=rs.at[n],
                device_id=(gx, gy + step, gz), device_id_type=MESH,
            )
            made.append((copy, to, origin))
        return made

    def fill_z(base, zr, arrays):
        for a in range(arrays):
            turned = jnp.concatenate([zr[0, a], jnp.zeros((sz - 16, rows_pad), F32), zr[1, a]], axis=0)
            base[a, :, :, sz:] = turned.T[0:rows].reshape(ex, ey, sz)

    keep_k = kmat.shape[0] == count
    block_i = 32

    def kernel_block(start):
        squared = None
        for component in range(3):
            offset = cols[pl.ds(start, block_i), component : component + 1] - listed[component : component + 1]
            squared = offset * offset if squared is None else squared + offset * offset
        return lax.rsqrt(squared + 1.0)

    def potentials(weights):
        def body(i, _):
            start = pl.multiple_of(i * block_i, block_i)
            block = kmat[pl.ds(start, block_i), :] if keep_k else kernel_block(start)
            value = jnp.sum(block * weights, axis=1, keepdims=True)
            cols[pl.ds(start, block_i), 4:5] = value
            z_id = cols[pl.ds(start, block_i), 2:3].astype(jnp.int32) - gy * sz
            z_id = jnp.where(z_id < 0, z_id + ez, z_id)
            lane = lax.broadcasted_iota(jnp.int32, (block_i, ez), 1)
            placed = jnp.where(lane == z_id, value, 0.0)
            high, low = split2(placed)
            spread[pl.ds(start, block_i), 0:ez] = high
            spread[pl.ds(start, block_i), ez:] = low
            return 0

        lax.fori_loop(0, count // block_i, body, 0)

    planes = 4

    def make_load():
        def body(i, _):
            start = pl.multiple_of(i * (planes * ey), 32)
            got = jnp.dot(onehot_ext[pl.ds(start, planes * ey), :], spread[...], preferred_element_type=F32)
            got = (got[:, 0:ez] + got[:, ez:]).reshape(planes, ey, ez)
            at = pl.ds(i * planes, planes)
            load[at] = (ext[1, at] + got) * inv[at]
            return 0

        lax.fori_loop(0, ex // planes, body, 0)

    def shifted(plane):
        return (
            pltpu.roll(plane, ey - 1, 0),
            pltpu.roll(plane, 1, 0),
            pltpu.roll(plane, ez - 1, 1),
            pltpu.roll(plane, 1, 1),
        )

    def make_coefficients():
        inv[0] = jnp.zeros((ey, ez), F32)
        inv[ex - 1] = jnp.zeros((ey, ez), F32)

        def body(x, _):
            middle = ext[2, x]
            others = (ext[2, x + 1], ext[2, x - 1]) + shifted(middle)
            faces = [0.5 * (middle + other) for other in others]
            diagonal = faces[0]
            for face in faces[1:]:
                diagonal = diagonal + face
            filled = middle > 0.0
            scale = jnp.where(filled, relax / jnp.where(filled, diagonal, 1.0), 0.0)
            inv[x] = scale
            for n, face in enumerate(faces):
                coef[n, x] = face * scale
            return 0

        lax.fori_loop(1, ex - 1, body, 0)

    def sweep(read, write, first, last, brick_only):
        def body(x, _):
            plane = read(x)
            values = (read(x + 1), read(x - 1)) + shifted(plane)
            if brick_only:
                cut = lambda array: array[0:sy, 0:sz]
                new = (1.0 - relax) * cut(plane) + load[x, 0:sy, 0:sz]
                for n, value in enumerate(values):
                    new = new + coef[n, x, 0:sy, 0:sz] * cut(value)
            else:
                new = (1.0 - relax) * plane + load[x]
                for n, value in enumerate(values):
                    new = new + coef[n, x] * value
            write(x, new)
            return 0

        lax.fori_loop(first, last, body, 0)

    def sweeps(start, write_last):
        reads = [start, lambda x: ping[x], lambda x: pong[x], lambda x: ping[x]]

        def to_ping(x, new):
            ping[x] = new

        def to_pong(x, new):
            pong[x] = new

        writes = [to_ping, to_pong, to_ping, write_last]
        for s in range(SWEEPS):
            sweep(reads[s], writes[s], s + 1, ex - s - 1, s == SWEEPS - 1)

    gather_weights(f_t, ws1_send.at[0])
    w1 = exchange_z(ws1_send.at[0], ws1.at[0], w1_ss.at[0], w1_rs.at[0])
    wait_halo(h1)
    fill_y(ext, yrecv, 3)
    h2 = z_copies(ext, zsend, zrecv, 3, h2_ss.at[0], h2_rs.at[0])
    start_halo(h2)
    w2 = w_stage2(0, w1)
    for n in range(count // 128):
        wide = jnp.concatenate([listed[:, n * 128 : (n + 1) * 128], jnp.zeros((120, 128), F32)], axis=0)
        cols[n * 128 : (n + 1) * 128, :] = wide.T
    if keep_k:

        def build(i, _):
            start = pl.multiple_of(i * block_i, block_i)
            kmat[pl.ds(start, block_i), :] = kernel_block(start)
            return 0

        lax.fori_loop(0, count // block_i, build, 0)
    fill_onehot(onehot_ext, row_ext, 32)
    wait_halo(h2)
    fill_z(ext, zrecv, 3)
    make_coefficients()
    potentials(w_total(0, w2))
    make_load()

    def to_ext2(x, new):
        ext2[0, x, 0:sy, 0:sz] = new

    sweeps(lambda x: ext[0, x], to_ext2)

    h1b = halo_copies(ext2, yrecv2, h1_ss.at[1], h1_rs.at[1])
    start_halo(h1b)
    gather_weights(brick_transposed(ext2), ws1_send.at[1])
    w1b = exchange_z(ws1_send.at[1], ws1.at[1], w1_ss.at[1], w1_rs.at[1])
    wait_halo(h1b)
    fill_y(ext2, yrecv2, 1)
    h2b = z_copies(ext2, zsend2, zrecv2, 1, h2_ss.at[1], h2_rs.at[1])
    start_halo(h2b)
    w2b = w_stage2(1, w1b)
    wait_halo(h2b)
    fill_z(ext2, zrecv2, 1)
    potentials(w_total(1, w2b))
    pot_ref[...] = cols[pl.ds(pl.multiple_of((q * gzn + gz) * own, own), own), 4:5]
    make_load()

    def to_out(x, new):
        out_ref[x - W] = new

    sweeps(lambda x: ext2[0, x], to_out)

    for copy in ag1_copies + ag2_copies + w1 + w2 + w1b + w2b:
        copy.wait_send()


def shards(source, conductance, field_start, panel_cell, panel_area):
    gxn, gyn, gzn = (lax.axis_size(name) for name in ("gx", "gy", "gz"))
    sx, sy, sz = field_start.shape
    own = panel_cell.shape[1]
    q_count = gxn * gyn
    width = own * gzn
    count = width * q_count
    cfg = (gxn, gyn, gzn, sx, sy, sz, own, count)
    panel = jnp.concatenate(
        [panel_cell.astype(F32), panel_area[None, :], jnp.zeros((4, own), F32)], axis=0
    )
    panel = jnp.tile(panel, (1, gzn))
    ex, ey, ez = sx + 2 * W, sy + 8, 2 * sz
    rows = ex * ey
    rows_pad = -(-rows // 128) * 128
    vmem = pltpu.VMEM
    dma = pltpu.SemaphoreType.DMA
    k_shape = (count, count) if count <= 1024 else (8, 128)
    scratch = [
        vmem((3, ex, ey, ez), F32),
        vmem((1, ex, ey, ez), F32),
        vmem((ex, ey, ez), F32),
        vmem((ex, ey, ez), F32),
        vmem((6, ex, ey, ez), F32),
        vmem((ex, ey, ez), F32),
        vmem((ex, ey, ez), F32),
        vmem((2, 3, ex, 8, sz), F32),
        vmem((2, 1, ex, 8, sz), F32),
        vmem((2, 3, 8, rows_pad), F32),
        vmem((2, 1, 8, rows_pad), F32),
        vmem((2, 3, 8, rows_pad), F32),
        vmem((2, 1, 8, rows_pad), F32),
        vmem((8, width), F32),
        vmem((gzn - 1, 8, width), F32),
        vmem((8, width), F32),
        vmem((q_count, 8, width), F32),
        vmem((2, q_count, width), F32),
        vmem((2, gzn - 1, q_count, width), F32),
        vmem((2, q_count, width), F32),
        vmem((2, q_count - 1, q_count, width), F32),
        vmem((count, 128), F32),
        vmem((sx * sy, count), BF16),
        vmem((rows, count), BF16),
        vmem((count, 2 * ez), BF16),
        vmem(k_shape, F32),
        dma((3,)),
        dma((gzn - 1,)), dma((gzn - 1,)),
        dma((q_count - 1,)), dma((q_count - 1,)),
        dma((2, 8)), dma((2, 8)),
        dma((2, 2)), dma((2, 2)),
        dma((2, gzn - 1)), dma((2, gzn - 1)),
        dma((2, q_count - 1)), dma((2, q_count - 1)),
    ]
    whole = pl.BlockSpec(memory_space=pltpu.VMEM)
    apart = pl.BlockSpec(memory_space=pl.ANY)
    field, potential = pl.pallas_call(
        functools.partial(kernel, cfg),
        out_shape=(
            jax.ShapeDtypeStruct((sx, sy, sz), F32),
            jax.ShapeDtypeStruct((own, 1), F32),
        ),
        in_specs=[whole, apart, apart, apart],
        out_specs=(whole, whole),
        scratch_shapes=scratch,
        compiler_params=pltpu.CompilerParams(
            collective_id=0, has_side_effects=True, vmem_limit_bytes=60 * 1024 * 1024
        ),
    )(panel, field_start, source, conductance)
    return field, potential.reshape(own)


def solution(mesh):
    in_specs = (
        P("gx", "gz", "gy"),
        P("gx", "gz", "gy"),
        P("gx", "gz", "gy"),
        P(None, ("gx", "gy", "gz")),
        P(("gx", "gy", "gz")),
    )
    out_specs = (P("gx", "gz", "gy"), P(("gx", "gy", "gz")))
    return jax.shard_map(shards, mesh=mesh, in_specs=in_specs, out_specs=out_specs, check_vma=False)
```

time: 477 us -> 72.4 us (0.15); the launches traced: 470 us -> 72.1 us
  blocking collectives: 235 us -> 0 us
  starting transfers between devices: 150 us -> 0 us
  Pallas kernels: 0 us -> 66.4 us
  waiting for transfers between devices: 41.6 us -> 0 us
  other arithmetic: 24 us -> 1.42 us
  local copies, waits for them, and re-layouts: 17.1 us -> 3.67 us
    ppermute x54 -> x0, starting transfers between devices: 150 us -> none  [the longest x27 115 us: extended(): before = lax.ppermute(last, axis, up)]
    unnamed x2 -> x0, blocking collectives: 85.8 us -> none
    psum x2 -> x0, blocking collectives: 80.6 us -> none  [shards(): weights = lax.psum(weighted, ('gx', 'gy', 'gz'))]
    all_gather x1 -> x0, blocking collectives: 68.7 us -> none  [shards(): lax.all_gather(jnp.concatenate([own_xyz, panel_area[None, :]], 0), ('gx',...]
    pallas_call x0 -> x1, Pallas kernels: none -> 66.4 us  [shards(): pl.pallas_call(functools.partial(kernel, cfg), out_shape=(jax.ShapeDtypeS...]
    ppermute x54 -> x0, waiting for transfers between devices: 41.6 us -> none  [the longest x27 24.5 us: extended(): after = lax.ppermute(initial, axis, down)]
    scatter-add x2 -> x0, other arithmetic: 14.9 us -> none  [shards(): load = source.reshape(-1).at[flat_index].add(added).reshape(source.shape)]
    gather x2 -> x0, local copies, waits for them, and re-layouts: 12.3 us -> none  [shards(): picked = field.reshape(-1)[flat_index]]
  transfers between devices with their start and end apart: 54 -> 0, of which waited for: 18 -> 0; matrix products, arithmetic and copies ran while one was open for 6% -> 0% of each run, Pallas kernels for 0% -> 0%
where the time goes in v1:
time: 72.4 us; the launch traced here: 72.1 us
  Pallas kernels  66.4 us (92%)
  local copies, waits for them, and re-layouts  3.67 us (5%)
  other arithmetic  1.42 us (2%)
    pallas_call x1, Pallas kernels, shards(): pl.pallas_call(functools.partial(kernel, cfg), out_shape=(jax.ShapeDtypeS...  66.4 us
    unnamed x5, local copies, waits for them, and re-layouts  2.91 us

profile of v1, /device:TPU:0, one launch (start us, length us, event | category | flops | bytes accessed | tf_op | source)
XLA Modules:
  0.0 72.1 jit_solution(13146024722346908860)
XLA Ops:
  0.6 0.0 copy-start
  0.6 0.1 pad.2.clone
  0.7 0.6 copy-done
  1.3 0.0 copy-start.1
  1.3 0.7 copy-done.1
  2.0 0.1 maximum_maximum_fusion
  2.0 0.7 tile.10.panel_ref
  2.7 66.4 %shard_map.68 = (f32[16,32,128]{2,1,0:T(8,128)}, f32[32,1]{1,0:T(8,128)}) custom-call(f32[8,128]{1,0:T(8,128)} %tile.10.panel_ref, f32[16,32,128]{2,1,0:T(8,128)} %field_ref.1, f32[16,32,128]{2,1,0:T(8,128)} %source_ref.1, f32[16,32,128]{2,1,0:T(8,128)} %cond_ref.1), custom_call_target="tpu_custom_call" | custom-call | tf_op jit(solution)/shard_map/pallas_call | solution.py:474
  69.1 1.3 %reduce = f32[32]{0:T(128)} reduce(f32[32,1]{1,0:T(8,128)} %get-tuple-element.5, f32[]{:T(128)} %constant.2), dimensions={1}, to_apply=%get-tuple-element.5.reduce_sub_computation | reduce | bytes 260 | tf_op jit(solution)/shard_map/pallas_call | solution.py:474
  70.4 1.7 %copy.8 = f32[16,32,128]{2,1,0:T(8,128)} copy(f32[16,32,128]{2,1,0:T(8,128)} %get-tuple-element.8) | data formatting | bytes 524288
  (3 shorter events, 0.0 us)
Async XLA Ops:
  0.6 0.7 copy-start
  1.3 0.7 copy-start.1

commit v2 on v1

--- a/solution.py
+++ b/solution.py
@@ -190,7 +190,7 @@
             ref[pl.ds(start, block), :] = jnp.where(sub == ids, 1.0, 0.0).astype(BF16)
             return 0
 
-        lax.fori_loop(0, ref.shape[0] // block, body, 0)
+        lax.fori_loop(0, ref.shape[0] // block, body, 0, unroll=2)
 
     fill_onehot(onehot, row_id, 32)
 
@@ -264,7 +264,7 @@
             base[a, :, :, sz:] = turned.T[0:rows].reshape(ex, ey, sz)
 
     keep_k = kmat.shape[0] == count
-    block_i = 32
+    block_i = max(16, 131072 // count)
 
     def kernel_block(start):
         squared = None
@@ -290,7 +290,7 @@
 
         lax.fori_loop(0, count // block_i, body, 0)
 
-    planes = 4
+    planes = ex // 2
 
     def make_load():
         def body(i, _):
@@ -329,7 +329,7 @@
                 coef[n, x] = face * scale
             return 0
 
-        lax.fori_loop(1, ex - 1, body, 0)
+        lax.fori_loop(1, ex - 1, body, 0, unroll=2)
 
     def sweep(read, write, first, last, brick_only):
         def body(x, _):
@@ -347,7 +347,7 @@
             write(x, new)
             return 0
 
-        lax.fori_loop(first, last, body, 0)
+        lax.fori_loop(first, last, body, 0, unroll=True)
 
     def sweeps(start, write_last):
         reads = [start, lambda x: ping[x], lambda x: pong[x], lambda x: ping[x]]
@@ -404,7 +404,9 @@
     wait_halo(h2b)
     fill_z(ext2, zrecv2, 1)
     potentials(w_total(1, w2b))
-    pot_ref[...] = cols[pl.ds(pl.multiple_of((q * gzn + gz) * own, own), own), 4:5]
+    row = cols[pl.ds(pl.multiple_of(q * width, width), width), :].T[4:5]
+    row = pltpu.roll(row, lax.rem(width - gz * own, width), 1)
+    pot_ref[...] = row[:, 0:own]
     make_load()
 
     def to_out(x, new):
@@ -475,7 +477,7 @@
         functools.partial(kernel, cfg),
         out_shape=(
             jax.ShapeDtypeStruct((sx, sy, sz), F32),
-            jax.ShapeDtypeStruct((own, 1), F32),
+            jax.ShapeDtypeStruct((1, own), F32),
         ),
         in_specs=[whole, apart, apart, apart],
         out_specs=(whole, whole),

time: 72.4 us -> 48.8 us (0.67)
  Pallas kernels: 66.4 us -> 43.7 us
  other arithmetic: 1.42 us -> 0.07 us
    pallas_call x1, Pallas kernels: 66.4 us -> 43.7 us  [shards(): pl.pallas_call(functools.partial(kernel, cfg), out_shape=(jax.ShapeDtypeS...]
    pallas_call x1 -> x0, other arithmetic: 1.35 us -> none  [shards(): pl.pallas_call(functools.partial(kernel, cfg), out_shape=(jax.ShapeDtypeS...]
    unnamed x5 -> x8, local copies, waits for them, and re-layouts: 2.91 us -> 3.43 us
where the time goes in v2:
time: 48.8 us; the launch traced here: 48.6 us
  Pallas kernels  43.7 us (90%)
  local copies, waits for them, and re-layouts  4.19 us (9%)
  between operations  0.67 us (1%)
    pallas_call x1, Pallas kernels, shards(): pl.pallas_call(functools.partial(kernel, cfg), out_shape=(jax.ShapeDtypeS...  43.7 us
    unnamed x8, local copies, waits for them, and re-layouts  3.43 us

profile of v2, /device:TPU:0, one launch (start us, length us, event | category | flops | bytes accessed | tf_op | source)
XLA Modules:
  0.0 48.6 jit_solution(690702419429231236)
XLA Ops:
  0.6 0.0 copy-start
  0.6 0.1 pad.2.clone
  0.7 0.6 %copy-done = s32[3,32]{1,0:T(4,128)S(1)} copy-done((s32[3,32]{1,0:T(4,128)S(1)}, s32[3,32]{1,0:T(4,128)}, u32[]{:S(2)}) %copy-start) | copy-done | bytes 408
  1.3 0.0 copy-start.1
  1.3 0.7 %copy-done.1 = f32[32]{0:T(128)S(1)} copy-done((f32[32]{0:T(128)S(1)}, f32[32]{0:T(128)}, u32[]{:S(2)}) %copy-start.1) | copy-done | bytes 152
  2.0 0.1 maximum_maximum_fusion
  2.0 0.7 %tile.10.panel_ref = f32[8,128]{1,0:T(8,128)} reshape(f32[8,4,32]{2,1,0:T(4,128)S(1)} %tile.4) | data formatting | bytes 8192 | tf_op jit(solution)/shard_map/tile | solution.py:432
  2.7 43.7 %shard_map.68 = (f32[16,32,128]{2,1,0:T(8,128)}, f32[1,32]{1,0:T(1,128)}) custom-call(f32[8,128]{1,0:T(8,128)} %tile.10.panel_ref, f32[16,32,128]{2,1,0:T(8,128)} %field_ref.1, f32[16,32,128]{2,1,0:T(8,128)} %source_ref.1, f32[16,32,128]{2,1,0:T(8,128)} %cond_ref.1), custom_call_target="tpu_custom_call" | custom-call | tf_op jit(solution)/shard_map/pallas_call | solution.py:476
  46.4 0.0 copy-start.2
  46.4 1.7 %copy.9 = f32[16,32,128]{2,1,0:T(8,128)} copy(f32[16,32,128]{2,1,0:T(8,128)} %get-tuple-element.8) | data formatting | bytes 524288
  48.1 0.0 copy-done.2
  48.1 0.5 %copy.10 = f32[32]{0:T(128)} copy(f32[32]{0:T(128)S(1)} %bitcast.3) | data formatting | bytes 256
  (3 shorter events, 0.0 us)
Async XLA Ops:
  0.6 0.7 %copy-start = (s32[3,32]{1,0:T(4,128)S(1)}, s32[3,32]{1,0:T(4,128)}, u32[]{:S(2)}) copy-start(s32[3,32]{1,0:T(4,128)} %param.8) | copy-start | bytes 1156
  1.3 0.7 %copy-start.1 = (f32[32]{0:T(128)S(1)}, f32[32]{0:T(128)}, u32[]{:S(2)}) copy-start(f32[32]{0:T(128)} %param.9) | copy-start | bytes 388
  46.4 1.7 %copy-start.2 = (f32[1,32]{1,0:T(1,128)S(1)}, f32[1,32]{1,0:T(1,128)}, u32[]{:S(2)}) copy-start(f32[1,32]{1,0:T(1,128)} %get-tuple-element.5) | copy-start | bytes 388
